TPU v7x, 32 devices: a whole 2x2x4 slice. The times are simulated.
32 devices in a mesh: seq: 8 (over z, core), chan: 4 (over y, x).
Axes of the slice: x: 2, y: 2, z: 4, core: 2. Of those that a mesh axis runs over, the one named last changes fastest.
Arguments:
- features: bfloat16 [3, 4096, 4096], P(None, ('seq', 'chan')), may hold values from -6 to 6
- short_weight: float32 [3, 3, 4096], replicated, may hold values from -3.5 to 3.5
- decay_rate: float32 [16, 4096], P(None, 'chan'), as said below
- residue: float32 [16, 4096], P(None, 'chan'), may hold values from -1.5 to 1.5
- skip_gain: float32 [4096], P('chan'), may hold values from 0.5 to 1.5
Outputs:
- mixed: bfloat16 [4096, 4096], P(('seq', 'chan'))
Inputs may be any that keep to these rules, and one draw needn't show every extreme that they name: `decay_rate`: every rate is positive and at most 1/30.
All inputs are finite; a program needn't handle non-finite values.
Results may differ from a plain program's by a relative error of at most 0.0075.
Values may be sent and summed in bfloat16 or wider, within the bound.
A program may use at most 128 MiB of HBM per device.

v0:
```python
import math

import jax
import jax.numpy as jnp
from jax import lax
from jax.sharding import PartitionSpec as P

block_len = 64


def from_behind(block, axis, distance):
    devices = range(lax.axis_size(axis))
    route = [(i - distance, i) for i in devices if i - distance in devices]
    return lax.ppermute(block, axis, route)


def short_filter(padded, weights, taps):
    length = padded.shape[1] - taps + 1
    total = jnp.zeros((padded.shape[0], length, padded.shape[2]), jnp.float32)
    for offset in range(taps):
        window = lax.slice_in_dim(
            padded, taps - 1 - offset, taps - 1 - offset + length, axis=1
        ).astype(jnp.float32)
        total = total + weights[:, offset, :][:, None, :] * window
    return total


def modal_tables(decay_rate, scaled_residue, block):
    positions = jnp.arange(block).astype(jnp.float32)
    kernel = jnp.sum(
        scaled_residue[:, None, :] * jnp.exp(-decay_rate[:, None, :] * positions[None, :, None]),
        axis=0,
    )
    lag_index = jnp.arange(block)[:, None] - jnp.arange(block)[None, :]
    one_hot = (lag_index[:, :, None] == jnp.arange(block)[None, None, :]).astype(jnp.float32)
    toeplitz = jnp.dot(
        one_hot.reshape(block * block, block), kernel, precision=lax.Precision.HIGHEST
    ).reshape(block, block, kernel.shape[1])
    ending = jnp.exp(-decay_rate[:, None, :] * (block - 1.0 - positions)[None, :, None])
    reading = scaled_residue[:, None, :] * jnp.exp(
        -decay_rate[:, None, :] * (positions + 1.0)[None, :, None]
    )
    return (toeplitz, ending, reading)


def modal_conv(signal, decay_rate, tables, start_state, block):
    toeplitz, ending, reading = tables
    count = signal.shape[0] // block
    pieces = signal.reshape(count, block, signal.shape[1])
    inner = jnp.einsum("ijc,kjc->kic", toeplitz, pieces, precision=lax.Precision.HIGHEST)
    local_end = jnp.einsum("njc,kjc->knc", ending, pieces, precision=lax.Precision.HIGHEST)
    group_decay = jnp.exp(-decay_rate * block)

    def advance(state, piece):
        return (group_decay * state + piece, state)

    final, starts = lax.scan(advance, start_state, local_end)
    carried = jnp.einsum("nic,knc->kic", reading, starts, precision=lax.Precision.HIGHEST)
    return ((inner + carried).reshape(signal.shape), final)


def long_part(product, decay_rate, residue, skip_gain):
    signal = product.astype(jnp.float32)
    section = signal.shape[0]
    block = math.gcd(section, block_len)
    count = section // block
    scaled = residue * jnp.sqrt(1.0 - jnp.exp(-2.0 * decay_rate))
    tables = modal_tables(decay_rate, scaled, block)
    zero_state = jnp.zeros_like(decay_rate)
    longconv, end_state = modal_conv(signal, decay_rate, tables, zero_state, block)
    section_decay = jnp.exp(-decay_rate * section)

    def advance_section(turn_index, carry_state):
        return from_behind(section_decay * carry_state + end_state, "seq", 1)

    incoming = lax.fori_loop(0, lax.axis_size("seq") - 1, advance_section, zero_state)
    block_starts = (jnp.arange(count).astype(jnp.float32) * block)[:, None, None]
    entering = jnp.exp(-decay_rate[None, :, :] * block_starts) * incoming[None, :, :]
    correction = jnp.einsum(
        "nic,knc->kic", tables[2], entering, precision=lax.Precision.HIGHEST
    ).reshape(signal.shape)
    return (longconv + correction + skip_gain[None, :] * signal).astype(jnp.bfloat16)


def local(features, short_weight, decay_rate, residue, skip_gain):
    taps = short_weight.shape[1]
    chan_width = decay_rate.shape[1]
    columns = lax.all_to_all(features, "chan", split_axis=2, concat_axis=1, tiled=True)
    border = from_behind(columns[:, columns.shape[1] - (taps - 1) :, :], "seq", 1)
    weights = lax.dynamic_slice_in_dim(
        short_weight, lax.axis_index("chan") * chan_width, chan_width, 2
    )
    padded = jnp.concatenate([border, columns], axis=1)
    filtered = lax.optimization_barrier(short_filter(padded, weights, taps).astype(jnp.bfloat16))
    product = lax.optimization_barrier(
        (filtered[1].astype(jnp.float32) * filtered[2].astype(jnp.float32)).astype(jnp.bfloat16)
    )
    conv_out = lax.optimization_barrier(long_part(product, decay_rate, residue, skip_gain))
    gated = (filtered[0].astype(jnp.float32) * conv_out.astype(jnp.float32)).astype(jnp.bfloat16)
    return lax.all_to_all(gated, "chan", split_axis=0, concat_axis=1, tiled=True)


def solution(mesh):
    return jax.shard_map(
        local,
        mesh=mesh,
        in_specs=(P(None, ("seq", "chan"), None), P(), P(None, "chan"), P(None, "chan"), P("chan")),
        out_specs=P(("seq", "chan"), None),
        check_vma=False,
    )
```

profile of v0, /device:TPU:0, one launch (start us, length us, event | category | flops | bytes accessed | tf_op | source)
XLA Modules:
  0.0 234.7 jit_solution(10474530480859475976)
XLA Ops:
  0.0 7.2 %copy.25 = bf16[3,128,4096]{1,0,2:T(4,128)(2,1)} copy(bf16[3,128,4096]{2,1,0:T(8,128)(2,1)} %param.9) | data formatting | bytes 6291456 | tf_op args[0]
  7.2 5.3 %all-to-all-start = ((bf16[3,128,4096]{1,0,2:T(4,128)(2,1)}), bf16[3,128,4096]{1,0,2:T(4,128)(2,1)}, u32[]{:S(2)}, u32[]{:S(2)}) async-start(bf16[3,128,4096]{1,0,2:T(4,128)(2,1)} %copy.25), calls=%async_computation | async-start | bytes 8388608 | tf_op jit(solution)/shard_map/all_to_all | solution.py:88
  12.5 0.1 multiply_exponential_fusion.1
  12.6 0.2 copy.28
  12.8 0.0 copy-start.3
  12.8 0.2 copy.27
  13.1 1.1 constant_dynamic-slice_fusion.1
  14.2 11.8 %multiply_reduce_fusion = f32[64,1024]{0,1:T(8,128)S(1)} fusion(f32[64]{0:T(128)S(1)} %iota_convert_fusion, f32[16,1024]{0,1:T(8,128)S(1)} %copy.28, f32[16,1024]{0,1:T(8,128)S(1)} %copy.27), kind=kLoop, calls=%fused_computation.9 | loop fusion | flops 3080192 | bytes 393472 | tf_op jit(solution)/shard_map/reduce_sum | solution.py:30
  26.0 10.2 %fusion.25 = f32[64,64,1024]{2,1,0:T(8,128)} fusion(s32[64,64]{1,0:T(8,128)S(1)} %iota_subtract_fusion, f32[64,1024]{0,1:T(8,128)S(1)} %multiply_reduce_fusion), kind=kOutput, calls=%fused_computation.37 | convolution fusion | flops 3221487616 | bytes 17055744 | tf_op jit(solution)/shard_map/dot_general | solution.py:36
  36.2 24.9 %all-to-all-done = bf16[3,128,4096]{1,0,2:T(4,128)(2,1)} async-done(((bf16[3,128,4096]{1,0,2:T(4,128)(2,1)}), bf16[3,128,4096]{1,0,2:T(4,128)(2,1)}, u32[]{:S(2)}, u32[]{:S(2)}) %all-to-all-start) | async-done | bytes 3145760 | tf_op jit(solution)/shard_map/all_to_all | solution.py:88
  61.1 5.5 %copy.26 = bf16[3,128,4,1024]{3,1,2,0:T(8,128)(2,1)S(1)} copy(bf16[3,128,4,1024]{1,0,3,2:T(4,128)(2,1)} %bitcast) | data formatting | bytes 6291456 | tf_op jit(solution)/shard_map/all_to_all | solution.py:88
  66.6 1.5 collective-permute-start.1
  68.2 30.5 %copy.31 = f32[64,64,1024]{1,0,2:T(8,128)} copy(f32[64,64,1024]{2,1,0:T(8,128)} %fusion.25) | data formatting | bytes 33554432 | tf_op jit(solution)/shard_map/dot_general | solution.py:36
  98.7 0.0 collective-permute-done.1
  98.7 2.4 %add_convert_fusion = bf16[3,512,1024]{2,1,0:T(8,128)(2,1)S(1)} fusion(bf16[3,512,1024]{2,1,0:T(8,128)(2,1)S(1)} %bitcast.47, bf16[3,2,1024]{2,1,0:T(2,128)(2,1)S(1)} %collective-permute-done.1, f32[3,1024]{1,0:T(4,128)S(1)} %get-tuple-element.116, f32[3,1024]{1,0:T(4,128)S(1)} %get-tuple-element.117, f32[3,1024]{1,0:T(4,128)S(1)} %bitcast.51), kind=kLoop, calls=%fused_computation.10 | loop fusion | flops 23592960 | bytes 6340608 | tf_op jit(solution)/shard_map/convert_element_type | solution.py:94
  101.1 0.4 fusion.26
  101.5 1.2 copy-done.2
  102.7 1.7 copy.30
  104.4 0.0 copy-start.4
  104.4 30.9 %fusion.29 = f32[1024,8,64]{2,1,0:T(8,128)} fusion(bf16[8,64,1024]{1,0,2:T(8,128)(2,1)S(1)} %copy.30, f32[64,64,1024]{1,0,2:T(8,128)} %copy.31), kind=kOutput, calls=%fused_computation.56 | convolution fusion | flops 402653184 | bytes 19922944 | tf_op jit(solution)/shard_map/ijc,kjc->kic/dot_general | solution.py:50
  135.3 9.3 %fusion.17 = f32[8,16,1024]{1,0,2:T(8,128)} fusion(bf16[8,64,1024]{1,0,2:T(8,128)(2,1)S(1)} %copy.30, f32[64]{0:T(128)S(1)} %broadcast_subtract_fusion, f32[16,1024]{0,1:T(8,128)S(1)} %copy-done.4), kind=kOutput, calls=%fused_computation.27 | convolution fusion | flops 101711872 | bytes 1638656 | tf_op jit(solution)/shard_map/njc,kjc->knc/dot_general | solution.py:51
  144.7 2.8 %copy.33 = f32[8,16,1024]{2,1,0:T(8,128)S(1)} copy(f32[8,16,1024]{1,0,2:T(8,128)} %fusion.17) | data formatting | bytes 1048576
  147.5 0.0 copy-start.5
  147.6 0.5 while.24
  148.1 36.6 %while.23 = (s32[]{:T(128)}, f32[16,1024]{1,0:T(8,128)S(1)}, f32[16,1024]{1,0:T(8,128)S(1)}, f32[16,1024]{1,0:T(8,128)S(1)}, s32[]{:T(128)}) while((s32[]{:T(128)}, f32[16,1024]{1,0:T(8,128)S(1)}, f32[16,1024]{1,0:T(8,128)S(1)}, f32[16,1024]{1,0:T(8,128)S(1)}, s32[]{:T(128)}) %tuple.47), condition=%wide.region_4.5_spmd, body=%wide.region_3.4_spmd.sunk | while | flops 32770 | bytes 524389 | solution.py:76
  148.1 4.5 %collective-permute-start = (f32[16,1024]{1,0:T(8,128)S(1)}, f32[16,1024]{1,0:T(8,128)S(1)}, u32[]{:S(2)}, u32[]{:S(2)}) collective-permute-start(f32[16,1024]{1,0:T(8,128)S(1)} %multiply_add_fusion.2), channel_id=1, source_target_pairs={{0,4},{4,8},{8,12},{12,16},{16,20},{20,24},{24,28},{1,5},{5,9},{9,... | collective-permute-start | bytes 196616 | tf_op jit(solution)/shard_map/while/body/eval_jaxpr/ppermute | solution.py:14
  152.6 0.9 collective-permute-done
  153.5 2.3 %collective-permute-start = (f32[16,1024]{1,0:T(8,128)S(1)}, f32[16,1024]{1,0:T(8,128)S(1)}, u32[]{:S(2)}, u32[]{:S(2)}) collective-permute-start(f32[16,1024]{1,0:T(8,128)S(1)} %multiply_add_fusion.2), channel_id=1, source_target_pairs={{0,4},{4,8},{8,12},{12,16},{16,20},{20,24},{24,28},{1,5},{5,9},{9,... | collective-permute-start | bytes 196616 | tf_op jit(solution)/shard_map/while/body/eval_jaxpr/ppermute | solution.py:14
  155.8 0.9 collective-permute-done
  156.7 4.7 %collective-permute-start = (f32[16,1024]{1,0:T(8,128)S(1)}, f32[16,1024]{1,0:T(8,128)S(1)}, u32[]{:S(2)}, u32[]{:S(2)}) collective-permute-start(f32[16,1024]{1,0:T(8,128)S(1)} %multiply_add_fusion.2), channel_id=1, source_target_pairs={{0,4},{4,8},{8,12},{12,16},{16,20},{20,24},{24,28},{1,5},{5,9},{9,... | collective-permute-start | bytes 196616 | tf_op jit(solution)/shard_map/while/body/eval_jaxpr/ppermute | solution.py:14
  161.4 0.9 collective-permute-done
  162.3 4.7 %collective-permute-start = (f32[16,1024]{1,0:T(8,128)S(1)}, f32[16,1024]{1,0:T(8,128)S(1)}, u32[]{:S(2)}, u32[]{:S(2)}) collective-permute-start(f32[16,1024]{1,0:T(8,128)S(1)} %multiply_add_fusion.2), channel_id=1, source_target_pairs={{0,4},{4,8},{8,12},{12,16},{16,20},{20,24},{24,28},{1,5},{5,9},{9,... | collective-permute-start | bytes 196616 | tf_op jit(solution)/shard_map/while/body/eval_jaxpr/ppermute | solution.py:14
  167.1 0.9 collective-permute-done
  167.9 4.7 %collective-permute-start = (f32[16,1024]{1,0:T(8,128)S(1)}, f32[16,1024]{1,0:T(8,128)S(1)}, u32[]{:S(2)}, u32[]{:S(2)}) collective-permute-start(f32[16,1024]{1,0:T(8,128)S(1)} %multiply_add_fusion.2), channel_id=1, source_target_pairs={{0,4},{4,8},{8,12},{12,16},{16,20},{20,24},{24,28},{1,5},{5,9},{9,... | collective-permute-start | bytes 196616 | tf_op jit(solution)/shard_map/while/body/eval_jaxpr/ppermute | solution.py:14
  172.7 0.9 collective-permute-done
  173.5 4.7 %collective-permute-start = (f32[16,1024]{1,0:T(8,128)S(1)}, f32[16,1024]{1,0:T(8,128)S(1)}, u32[]{:S(2)}, u32[]{:S(2)}) collective-permute-start(f32[16,1024]{1,0:T(8,128)S(1)} %multiply_add_fusion.2), channel_id=1, source_target_pairs={{0,4},{4,8},{8,12},{12,16},{16,20},{20,24},{24,28},{1,5},{5,9},{9,... | collective-permute-start | bytes 196616 | tf_op jit(solution)/shard_map/while/body/eval_jaxpr/ppermute | solution.py:14
  178.3 0.9 collective-permute-done
  179.1 4.7 %collective-permute-start = (f32[16,1024]{1,0:T(8,128)S(1)}, f32[16,1024]{1,0:T(8,128)S(1)}, u32[]{:S(2)}, u32[]{:S(2)}) collective-permute-start(f32[16,1024]{1,0:T(8,128)S(1)} %multiply_add_fusion.2), channel_id=1, source_target_pairs={{0,4},{4,8},{8,12},{12,16},{16,20},{20,24},{24,28},{1,5},{5,9},{9,... | collective-permute-start | bytes 196616 | tf_op jit(solution)/shard_map/while/body/eval_jaxpr/ppermute | solution.py:14
  183.9 0.9 collective-permute-done
  184.7 1.0 copy.36
  185.7 2.6 %copy.34 = f32[8,16,1024]{1,0,2:T(8,128)} copy(f32[8,16,1024]{2,1,0:T(8,128)S(1)} %get-tuple-element.55) | data formatting | bytes 1048576 | tf_op jit(solution)/shard_map/while | solution.py:57
  188.4 10.9 %fusion = f32[1024,8,64]{2,1,0:T(8,128)S(1)} fusion(f32[64]{0:T(128)S(1)} %broadcast_add_fusion, f32[16,1024]{0,1:T(8,128)S(1)} %copy-done.5, f32[16,1024]{0,1:T(8,128)S(1)} %copy-done.7, f32[16,1024]{0,1:T(8,128)S(1)} %copy-done.9, f32[8]{0:T(128)S(1)} %convert_multiply_fusion.1), kind=kOutput, calls=%fused_computation.4 | convolution fusion | flops 103022592 | bytes 2294048 | tf_op jit(solution)/shard_map/nic,knc->kic/dot_general | solution.py:79
  199.4 13.5 %add_bitcast_fusion = f32[8,64,1024]{1,0,2:T(8,128)} fusion(f32[1024,8,64]{2,1,0:T(8,128)S(1)} %fusion, f32[1024,8,64]{2,1,0:T(8,128)S(1)} %copy-done, f32[8,16,1024]{1,0,2:T(8,128)S(1)} %copy-done.1, f32[64]{0:T(128)S(1)} %broadcast_add_fusion, f32[16,1024]{0,1:T(8,128)S(1)} %copy-done.5, f32[16,1024]{0,1:T(8,128)S(1)} %copy-done.7), kind=kOutput, calls=%fused_computation.11 | convolution fusion | flops 103809024 | bytes 6947072 | tf_op jit(solution)/shard_map/nic,knc->kic/dot_general | solution.py:58
  212.8 2.8 %copy.37 = f32[8,64,1024]{2,1,0:T(8,128)S(1)} copy(f32[8,64,1024]{1,0,2:T(8,128)} %add_bitcast_fusion) | data formatting | bytes 4194304 | tf_op jit(solution)/shard_map/add | solution.py:82
  215.7 0.4 fusion.21
  216.1 1.6 fusion.20
  217.7 16.0 %all_to_all.37 = bf16[4,128,1024]{2,1,0:T(8,128)(2,1)S(1)} all-to-all(bf16[4,128,1024]{2,1,0:T(8,128)(2,1)S(1)} %bitcast.49), channel_id=1, replica_groups=mesh['seq'=8,'chan'=4] {'chan'}, dimensions={0} | all-to-all | bytes 2097152 | tf_op jit(solution)/shard_map/all_to_all | solution.py:100
  233.7 1.1 copy.44
  (56 shorter events, 0.5 us)
Async XLA Ops:
  7.2 5.3 %copy-start.10 = (f32[16,1024]{1,0:T(8,128)S(1)}, f32[16,1024]{1,0:T(8,128)}, u32[]{:S(2)}) copy-start(f32[16,1024]{1,0:T(8,128)} %param.11) | copy-start | bytes 196612
  7.2 5.3 %copy-start.11 = (f32[16,1024]{1,0:T(8,128)S(1)}, f32[16,1024]{1,0:T(8,128)}, u32[]{:S(2)}) copy-start(f32[16,1024]{1,0:T(8,128)} %param.12) | copy-start | bytes 196612
  7.2 53.9 %all-to-all-start = ((bf16[3,128,4096]{1,0,2:T(4,128)(2,1)}), bf16[3,128,4096]{1,0,2:T(4,128)(2,1)}, u32[]{:S(2)}, u32[]{:S(2)}) async-start(bf16[3,128,4096]{1,0,2:T(4,128)(2,1)} %copy.25), calls=%async_computation | async-start | bytes 8388608 | tf_op jit(solution)/shard_map/all_to_all | solution.py:88
  12.8 23.4 %copy-start.3 = (f32[16,1024]{0,1:T(8,128)}, f32[16,1024]{0,1:T(8,128)S(1)}, u32[]{:S(2)}) copy-start(f32[16,1024]{0,1:T(8,128)S(1)} %copy.28) | copy-start | bytes 196612
  13.0 23.2 %copy-start.6 = (f32[16,1024]{0,1:T(8,128)}, f32[16,1024]{0,1:T(8,128)S(1)}, u32[]{:S(2)}) copy-start(f32[16,1024]{0,1:T(8,128)S(1)} %copy.27) | copy-start | bytes 196612
  66.6 32.0 %collective-permute-start.1 = (bf16[3,2,1024]{2,1,0:T(2,128)(2,1)S(1)}, bf16[3,2,1024]{2,1,0:T(2,128)(2,1)S(1)}, u32[]{:S(2)}, u32[]{:S(2)}) collective-permute-start(bf16[3,2,1024]{2,1,0:T(2,128)(2,1)S(1)} %slice.36), channel_id=1, source_target_pairs={{0,4},{4,8},{8,12},{12,16},{16,20},{20,24},{24,28},{1,5},{5,9},{9,... | collective-permute-start | bytes 36872 | tf_op jit(solution)/shard_map/ppermute | solution.py:14
  101.1 1.6 copy-start.2
  104.4 30.9 %copy-start.4 = (f32[16,1024]{0,1:T(8,128)S(1)}, f32[16,1024]{0,1:T(8,128)}, u32[]{:S(2)}) copy-start(f32[16,1024]{0,1:T(8,128)} %copy-done.3) | copy-start | bytes 196612
  144.7 2.9 %copy-start.8 = (f32[8,16,1024]{2,1,0:T(8,128)S(1)}, f32[8,16,1024]{2,1,0:T(8,128)}, u32[]{:S(2)}) copy-start(f32[8,16,1024]{2,1,0:T(8,128)} %custom-call.1) | copy-start | bytes 1572868
  147.5 40.8 %copy-start.5 = (f32[16,1024]{0,1:T(8,128)S(1)}, f32[16,1024]{0,1:T(8,128)}, u32[]{:S(2)}) copy-start(f32[16,1024]{0,1:T(8,128)} %copy-done.3) | copy-start | bytes 196612
  147.6 40.8 %copy-start.7 = (f32[16,1024]{0,1:T(8,128)S(1)}, f32[16,1024]{0,1:T(8,128)}, u32[]{:S(2)}) copy-start(f32[16,1024]{0,1:T(8,128)} %copy-done.6) | copy-start | bytes 196612
  148.1 5.3 %collective-permute-start = (f32[16,1024]{1,0:T(8,128)S(1)}, f32[16,1024]{1,0:T(8,128)S(1)}, u32[]{:S(2)}, u32[]{:S(2)}) collective-permute-start(f32[16,1024]{1,0:T(8,128)S(1)} %multiply_add_fusion.2), channel_id=1, source_target_pairs={{0,4},{4,8},{8,12},{12,16},{16,20},{20,24},{24,28},{1,5},{5,9},{9,... | collective-permute-start | bytes 196616 | tf_op jit(solution)/shard_map/while/body/eval_jaxpr/ppermute | solution.py:14
  153.5 3.2 %collective-permute-start = (f32[16,1024]{1,0:T(8,128)S(1)}, f32[16,1024]{1,0:T(8,128)S(1)}, u32[]{:S(2)}, u32[]{:S(2)}) collective-permute-start(f32[16,1024]{1,0:T(8,128)S(1)} %multiply_add_fusion.2), channel_id=1, source_target_pairs={{0,4},{4,8},{8,12},{12,16},{16,20},{20,24},{24,28},{1,5},{5,9},{9,... | collective-permute-start | bytes 196616 | tf_op jit(solution)/shard_map/while/body/eval_jaxpr/ppermute | solution.py:14
  156.7 5.6 %collective-permute-start = (f32[16,1024]{1,0:T(8,128)S(1)}, f32[16,1024]{1,0:T(8,128)S(1)}, u32[]{:S(2)}, u32[]{:S(2)}) collective-permute-start(f32[16,1024]{1,0:T(8,128)S(1)} %multiply_add_fusion.2), channel_id=1, source_target_pairs={{0,4},{4,8},{8,12},{12,16},{16,20},{20,24},{24,28},{1,5},{5,9},{9,... | collective-permute-start | bytes 196616 | tf_op jit(solution)/shard_map/while/body/eval_jaxpr/ppermute | solution.py:14
  162.3 5.6 %collective-permute-start = (f32[16,1024]{1,0:T(8,128)S(1)}, f32[16,1024]{1,0:T(8,128)S(1)}, u32[]{:S(2)}, u32[]{:S(2)}) collective-permute-start(f32[16,1024]{1,0:T(8,128)S(1)} %multiply_add_fusion.2), channel_id=1, source_target_pairs={{0,4},{4,8},{8,12},{12,16},{16,20},{20,24},{24,28},{1,5},{5,9},{9,... | collective-permute-start | bytes 196616 | tf_op jit(solution)/shard_map/while/body/eval_jaxpr/ppermute | solution.py:14
  167.9 5.6 %collective-permute-start = (f32[16,1024]{1,0:T(8,128)S(1)}, f32[16,1024]{1,0:T(8,128)S(1)}, u32[]{:S(2)}, u32[]{:S(2)}) collective-permute-start(f32[16,1024]{1,0:T(8,128)S(1)} %multiply_add_fusion.2), channel_id=1, source_target_pairs={{0,4},{4,8},{8,12},{12,16},{16,20},{20,24},{24,28},{1,5},{5,9},{9,... | collective-permute-start | bytes 196616 | tf_op jit(solution)/shard_map/while/body/eval_jaxpr/ppermute | solution.py:14
  173.5 5.6 %collective-permute-start = (f32[16,1024]{1,0:T(8,128)S(1)}, f32[16,1024]{1,0:T(8,128)S(1)}, u32[]{:S(2)}, u32[]{:S(2)}) collective-permute-start(f32[16,1024]{1,0:T(8,128)S(1)} %multiply_add_fusion.2), channel_id=1, source_target_pairs={{0,4},{4,8},{8,12},{12,16},{16,20},{20,24},{24,28},{1,5},{5,9},{9,... | collective-permute-start | bytes 196616 | tf_op jit(solution)/shard_map/while/body/eval_jaxpr/ppermute | solution.py:14
  179.1 5.6 %collective-permute-start = (f32[16,1024]{1,0:T(8,128)S(1)}, f32[16,1024]{1,0:T(8,128)S(1)}, u32[]{:S(2)}, u32[]{:S(2)}) collective-permute-start(f32[16,1024]{1,0:T(8,128)S(1)} %multiply_add_fusion.2), channel_id=1, source_target_pairs={{0,4},{4,8},{8,12},{12,16},{16,20},{20,24},{24,28},{1,5},{5,9},{9,... | collective-permute-start | bytes 196616 | tf_op jit(solution)/shard_map/while/body/eval_jaxpr/ppermute | solution.py:14
  185.7 2.6 %copy-start.9 = (f32[16,1024]{0,1:T(8,128)S(1)}, f32[16,1024]{0,1:T(8,128)}, u32[]{:S(2)}) copy-start(f32[16,1024]{0,1:T(8,128)} %copy.36) | copy-start | bytes 196612
  188.4 11.0 %copy-start = (f32[1024,8,64]{2,1,0:T(8,128)S(1)}, f32[1024,8,64]{2,1,0:T(8,128)}, u32[]{:S(2)}) copy-start(f32[1024,8,64]{2,1,0:T(8,128)} %fusion.29) | copy-start | bytes 6291460
  188.4 11.0 %copy-start.1 = (f32[8,16,1024]{1,0,2:T(8,128)S(1)}, f32[8,16,1024]{1,0,2:T(8,128)}, u32[]{:S(2)}) copy-start(f32[8,16,1024]{1,0,2:T(8,128)} %copy.34) | copy-start | bytes 1572868
  212.8 2.9 %copy-start.12 = (f32[1024]{0:T(1024)S(1)}, f32[1024]{0:T(1024)}, u32[]{:S(2)}) copy-start(f32[1024]{0:T(1024)} %param.13) | copy-start | bytes 12292
where the time goes:
time: 239 us; the launch traced here: 235 us
  matrix products  74.9 us (31%)
  local copies, waits for them, and re-layouts  58.1 us (24%)
  starting transfers between devices  37.1 us (16%)
  waiting for transfers between devices  31.1 us (13%)
  other arithmetic  17 us (7%)
  blocking collectives  16 us (7%)
    ppermute x8, starting transfers between devices, from_behind(): return lax.ppermute(block, axis, route)  31.8 us
    dot_general x1, matrix products, modal_conv(): jnp.einsum('ijc,kjc->kic', toeplitz, pieces, precision=lax.Precision.HIGH...  30.9 us
    dot_general x1, local copies, waits for them, and re-layouts, modal_tables(): jnp.dot(one_hot.reshape(block * block, block), kernel, precision=lax.Prec...  30.5 us
    all_to_all x1, waiting for transfers between devices, local(): lax.all_to_all(features, 'chan', split_axis=2, concat_axis=1, tiled=True)  24.9 us
    all_to_all x1, blocking collectives, local(): lax.all_to_all(gated, 'chan', split_axis=0, concat_axis=1, tiled=True)  16 us
    dot_general x1, matrix products, modal_conv(): jnp.einsum('nic,knc->kic', reading, starts, precision=lax.Precision.HIGHEST)  13.5 us
    reduce_sum x1, other arithmetic, modal_tables(): jnp.sum(scaled_residue[:, None, :] * jnp.exp(-decay_rate[:, None, :] * po...  11.8 us
    unnamed x30, local copies, waits for them, and re-layouts  11.3 us
  transfers between devices with their start and end apart: 9, of which 8 were waited for; matrix products, arithmetic and copies ran while one was open for 23% of the time, Pallas kernels for 0%

commit v1 on v0

v1 whole, which is shorter than its diff:
```python
import functools

import jax
import jax.numpy as jnp
import numpy as np
from jax import lax
from jax.experimental import pallas as pl
from jax.experimental.pallas import tpu as pltpu
from jax.sharding import PartitionSpec as P

MESH = pl.DeviceIdType.MESH
f32, bf16 = jnp.float32, jnp.bfloat16

NODES = 12
ROWS = 16


def node_places(block):
    j = np.arange(NODES)
    return (block - 1) / 2 * (1 - np.cos(np.pi * (2 * j + 1) / (2 * NODES)))


def cardinals(points, nodes):
    out = np.ones((NODES,) + points.shape)
    for j in range(NODES):
        for i in range(NODES):
            if i != j:
                out[j] *= (points - nodes[i]) / (nodes[j] - nodes[i])
    return out


def constant_tables(block):
    nodes = node_places(block)
    t = np.arange(block)
    lag = t[:, None] - t[None, :]
    toeplitz = np.where(lag >= 0, cardinals(np.abs(lag).astype(float), nodes), 0.0)
    toeplitz = toeplitz.transpose(1, 0, 2).reshape(block, NODES * block)
    basis = np.zeros((block, ROWS))
    basis[:, :NODES] = cardinals(t.astype(float), nodes).T
    moment = basis[::-1].T
    return toeplitz, moment, basis


def kernel(
    n_seq, n_chan, cores, feat_hbm, taps, decay, residue, skip, toeplitz, moment, basis, out,
    feat, prod, gate, y, gx, modes, starts, border, b_send, b_recv,
    g_all, m_send, m_recv, z_send, z_recv, h_send, h_recv,
    copy_sem, b_ss, b_rs, g_ss, g_rs, m_ss, m_rs, h_ss, h_rs, z_ss, z_rs,
):
    streams, block, width = feat.shape
    n_taps = taps.shape[1]
    members = n_chan * cores
    planes = n_seq // cores
    own_width = width // members
    chan_width = width // n_chan
    fold = b_send.shape[1]
    folds = width // fold
    nodes = [float(v) for v in node_places(block)]

    seq, chan = lax.axis_index("seq"), lax.axis_index("chan")
    plane, core = seq // cores, lax.rem(seq, cores)
    me = core * n_chan + chan

    def member(i):
        return (plane * cores + i // n_chan, lax.rem(i, n_chan))

    def columns(i):
        start = lax.rem(i, n_chan) * chan_width + (i // n_chan) * own_width
        return pl.ds(pl.multiple_of(start, own_width), own_width)

    def other(i):
        return lax.rem(me + i, members)

    for m in range(streams):
        pltpu.make_async_copy(feat_hbm.at[m], feat.at[m], copy_sem.at[m]).start()

    barrier = pltpu.get_barrier_semaphore()

    @pl.loop(1, members)
    def _(i):
        pl.semaphore_signal(barrier, inc=1, device_id=member(other(i)), device_id_type=MESH)

    @pl.loop(1, planes)
    def _(i):
        there = lax.rem(plane + i, planes) * cores + core
        pl.semaphore_signal(barrier, inc=1, device_id=(there, chan), device_id_type=MESH)

    enters = jnp.logical_and(me == 0, plane > 0)
    leaves = jnp.logical_and(me == members - 1, plane < planes - 1)

    @pl.when(enters)
    def _():
        pl.semaphore_signal(
            barrier, inc=1, device_id=(plane * cores - 1, n_chan - 1), device_id_type=MESH)

    @pl.when(leaves)
    def _():
        pl.semaphore_signal(
            barrier, inc=1, device_id=((plane + 1) * cores, 0), device_id_type=MESH)

    own = pl.ds(pl.multiple_of(core * own_width, own_width), own_width)
    rate = decay[:, own]
    scaled = residue[:, own] * jnp.sqrt(1.0 - jnp.exp(-2.0 * rate))
    rows = []
    for j in range(NODES):
        a = jnp.exp(-rate * nodes[j])
        modes[j] = a
        rows.append(jnp.sum(scaled * a, axis=0, keepdims=True))
    gain = skip[:, own]
    gain_top = gain.astype(bf16).astype(f32)
    rows += [gain_top, gain - gain_top]
    rows += [jnp.zeros_like(gain)] * (ROWS - len(rows))
    g_all[me] = jnp.concatenate(rows, axis=0).astype(bf16)

    for m in range(streams):
        pltpu.make_async_copy(feat_hbm.at[m], feat.at[m], copy_sem.at[m]).wait()
    rows = []
    for m in range(streams):
        last = feat[m, block - 16:, :].astype(f32)
        for k in range(n_taps - 1):
            row = 16 - (n_taps - 1) + k
            rows += [last[row:row + 1, f * fold:(f + 1) * fold] for f in range(folds)]
    rows += [jnp.zeros_like(rows[0])] * (b_send.shape[0] - len(rows))
    b_send[...] = jnp.concatenate(rows, axis=0).astype(bf16)

    extra = jnp.where(enters, 1, 0) + jnp.where(leaves, 1, 0)
    pl.semaphore_wait(barrier, members - 1 + planes - 1 + extra)

    position = seq * n_chan + chan
    total = n_seq * n_chan
    after = lax.rem(position + 1, total)
    b_copy = pltpu.make_async_remote_copy(
        src_ref=b_send, dst_ref=b_recv, send_sem=b_ss, recv_sem=b_rs,
        device_id=(after // n_chan, lax.rem(after, n_chan)), device_id_type=MESH)

    @pl.when(position < total - 1)
    def _():
        b_copy.start()

    def g_copy(i, slot):
        return pltpu.make_async_remote_copy(
            src_ref=g_all.at[slot], dst_ref=g_all.at[slot], send_sem=g_ss.at[i],
            recv_sem=g_rs.at[slot], device_id=member(i), device_id_type=MESH)

    def m_copy(i, slot):
        return pltpu.make_async_remote_copy(
            src_ref=m_send.at[i], dst_ref=m_recv.at[slot], send_sem=m_ss.at[i],
            recv_sem=m_rs.at[slot], device_id=member(i), device_id_type=MESH)

    def h_copy(i, slot):
        return pltpu.make_async_remote_copy(
            src_ref=h_send.at[i], dst_ref=h_recv.at[slot], send_sem=h_ss.at[i],
            recv_sem=h_rs.at[slot], device_id=member(i), device_id_type=MESH)

    def z_copy(i, slot):
        return pltpu.make_async_remote_copy(
            src_ref=z_send, dst_ref=z_recv.at[slot], send_sem=z_ss.at[i],
            recv_sem=z_rs.at[slot], device_id=(i * cores + core, chan), device_id_type=MESH)

    @pl.loop(1, members)
    def _(i):
        g_copy(other(i), me).start()

    @pl.when(position > 0)
    def _():
        b_copy.wait_recv()
        got = b_recv[...].astype(f32)
        for m in range(streams):
            for k in range(n_taps - 1):
                for f in range(folds):
                    row = (m * (n_taps - 1) + k) * folds + f
                    border[m * (n_taps - 1) + k:m * (n_taps - 1) + k + 1,
                           f * fold:(f + 1) * fold] = got[row:row + 1]

    @pl.when(position == 0)
    def _():
        border[...] = jnp.zeros_like(border)

    top_row = lax.broadcasted_iota(jnp.int32, (8, own_width), 0)

    def short_filter(m, cols):
        x = feat[m, :, cols].astype(f32)
        total = taps[m, 0:1, cols] * x
        for j in range(1, n_taps):
            moved = pltpu.roll(x, j, 0)
            top = moved[:8]
            for k in range(j):
                place = m * (n_taps - 1) + n_taps - 1 - j + k
                top = jnp.where(top_row == k, border[place:place + 1, cols], top)
            moved = jnp.concatenate([top, moved[8:]], axis=0)
            total = total + taps[m, j:j + 1, cols] * moved
        return total.astype(bf16)

    @pl.loop(1, members + 1)
    def _(i):
        to = other(i)
        cols = columns(to)
        p = (short_filter(1, cols).astype(f32) * short_filter(2, cols).astype(f32)).astype(bf16)
        prod[:, cols] = p
        found = jnp.dot(moment[...], p, preferred_element_type=f32).astype(bf16)

        @pl.when(i < members)
        def _():
            m_send[to] = found
            m_copy(to, me).start()

        @pl.when(i == members)
        def _():
            m_recv[me] = found

    @pl.loop(0, members)
    def _(i):
        cols = columns(i)
        gate[:, cols] = short_filter(0, cols)

    block_decay = jnp.exp(-rate * block)

    @pl.loop(1, members)
    def _(i):
        m_copy(other(i), other(i)).wait_recv()

    def gather_block(b, state):
        starts[b] = state
        found = m_recv[b].astype(f32)
        state = block_decay * state
        for j in range(NODES):
            state = state + modes[j] * found[j:j + 1]
        return state

    final = lax.fori_loop(0, members, gather_block, jnp.zeros_like(rate))
    z_send[...] = final.astype(bf16)

    @pl.loop(plane + 1, planes)
    def _(i):
        z_copy(i, plane).start()

    @pl.loop(1, members)
    def _(i):
        g_copy(other(i), other(i)).wait_recv()

    @pl.loop(0, members)
    def _(i):
        cols = columns(i)
        p = prod[:, cols]
        g = g_all[i].astype(f32)
        for j in range(NODES):
            gx[j * block:(j + 1) * block, :] = (
                jnp.broadcast_to(g[j:j + 1], p.shape).astype(bf16) * p)
        inner = jnp.dot(toeplitz[...], gx[...], preferred_element_type=f32)
        both = g[NODES:NODES + 1] + g[NODES + 1:NODES + 2]
        y[:, cols] = inner + both * p.astype(f32)

    plane_decay = jnp.exp(-rate * (block * members))

    def gather_plane(i, state):
        z_copy(i, i).wait_recv()
        return plane_decay * state + z_recv[i].astype(f32)

    entering = lax.fori_loop(0, plane, gather_plane, jnp.zeros_like(rate))
    reading = scaled * jnp.exp(-rate)

    def respond(b, state):
        weighted = reading * (starts[b] + state)
        rows = [jnp.sum(modes[j] * weighted, axis=0, keepdims=True) for j in range(NODES)]
        rows += [jnp.zeros_like(rows[0])] * (ROWS - NODES)
        answer = jnp.concatenate(rows, axis=0).astype(bf16)

        @pl.when(b != me)
        def _():
            h_send[b] = answer
            h_copy(b, me).start()

        @pl.when(b == me)
        def _():
            h_recv[me] = answer

        return block_decay * state

    lax.fori_loop(0, members, respond, entering)

    @pl.loop(0, members)
    def _(i):
        at = other(i)
        cols = columns(at)

        @pl.when(i > 0)
        def _():
            h_copy(at, at).wait_recv()

        carried = jnp.dot(basis[...], h_recv[at], preferred_element_type=f32)
        conv = (y[:, cols] + carried).astype(bf16)
        out[:, cols] = (gate[:, cols].astype(f32) * conv.astype(f32)).astype(bf16)

    @pl.when(position < total - 1)
    def _():
        b_copy.wait_send()

    @pl.loop(1, members)
    def _(i):
        g_copy(other(i), me).wait_send()
        m_copy(other(i), me).wait_send()
        h_copy(other(i), me).wait_send()

    @pl.loop(plane + 1, planes)
    def _(i):
        z_copy(i, plane).wait_send()


def local(n_seq, n_chan, features, short_weight, decay_rate, residue, skip_gain):
    streams, block, width = features.shape
    modes = decay_rate.shape[0]
    cores = 2 if n_seq % 2 == 0 else 1
    members = n_chan * cores
    planes = n_seq // cores
    own_width = width // members
    halo = streams * (short_weight.shape[1] - 1)
    fold = width // 4
    halo_rows = -(-halo * 4 // 16) * 16
    toeplitz, moment, basis = constant_tables(block)
    vmem = pl.BlockSpec(memory_space=pltpu.VMEM)
    dma = pltpu.SemaphoreType.DMA
    small = pltpu.VMEM((members, ROWS, own_width), bf16)
    return pl.pallas_call(
        functools.partial(kernel, n_seq, n_chan, cores),
        out_shape=jax.ShapeDtypeStruct((block, width), bf16),
        in_specs=[pl.BlockSpec(memory_space=pl.ANY)] + [vmem] * 7,
        out_specs=vmem,
        scratch_shapes=[
            pltpu.VMEM((streams, block, width), bf16),
            pltpu.VMEM((block, width), bf16),
            pltpu.VMEM((block, width), bf16),
            pltpu.VMEM((block, width), f32),
            pltpu.VMEM((NODES * block, own_width), bf16),
            pltpu.VMEM((NODES, modes, own_width), f32),
            pltpu.VMEM((members, modes, own_width), f32),
            pltpu.VMEM((-(-halo // 8) * 8, width), f32),
            pltpu.VMEM((halo_rows, fold), bf16),
            pltpu.VMEM((halo_rows, fold), bf16),
            small, small, small,
            pltpu.VMEM((modes, own_width), bf16),
            pltpu.VMEM((planes, modes, own_width), bf16),
            small, small,
            dma((streams,)), dma, dma,
            dma((members,)), dma((members,)), dma((members,)), dma((members,)),
            dma((members,)), dma((members,)), dma((planes,)), dma((planes,)),
        ],
        compiler_params=pltpu.CompilerParams(
            collective_id=0, has_side_effects=True, vmem_limit_bytes=40 * 2**20),
        cost_estimate=pl.CostEstimate(
            flops=2 * block * NODES * block * width,
            bytes_accessed=8 * block * width, transcendentals=0),
    )(
        features, short_weight, decay_rate, residue, skip_gain.reshape(1, -1),
        jnp.asarray(toeplitz, bf16), jnp.asarray(moment, bf16), jnp.asarray(basis, bf16),
    )


def solution(mesh):
    return jax.shard_map(
        functools.partial(local, mesh.shape["seq"], mesh.shape["chan"]),
        mesh=mesh,
        in_specs=(P(None, ("seq", "chan"), None), P(), P(None, "chan"), P(None, "chan"), P("chan")),
        out_specs=P(("seq", "chan"), None),
        check_vma=False,
    )
```

time: 239 us -> 32.9 us (0.14); the launches traced: 235 us -> 32.5 us
  matrix products: 74.9 us -> 0 us
  local copies, waits for them, and re-layouts: 58.1 us -> 8.59 us
  starting transfers between devices: 37.1 us -> 0 us
  waiting for transfers between devices: 31.1 us -> 0 us
  Pallas kernels: 0 us -> 23.9 us
  other arithmetic: 17 us -> 0 us
  blocking collectives: 16 us -> 0 us
    dot_general x5 -> x0, matrix products: 74.9 us -> none  [the longest x1 30.9 us: modal_conv(): jnp.einsum('ijc,kjc->kic', toeplitz, pieces, precision=lax.Precision.HIGH...]
    ppermute x8 -> x0, starting transfers between devices: 31.8 us -> none  [from_behind(): return lax.ppermute(block, axis, route)]
    dot_general x1 -> x0, local copies, waits for them, and re-layouts: 30.5 us -> none  [modal_tables(): jnp.dot(one_hot.reshape(block * block, block), kernel, precision=lax.Prec...]
    all_to_all x1 -> x0, waiting for transfers between devices: 24.9 us -> none  [local(): lax.all_to_all(features, 'chan', split_axis=2, concat_axis=1, tiled=True)]
    pallas_call x0 -> x1, Pallas kernels: none -> 23.9 us  [local(): pl.pallas_call(functools.partial(kernel, n_seq, n_chan, cores), out_shape...]
    all_to_all x1 -> x0, blocking collectives: 16 us -> none  [local(): lax.all_to_all(gated, 'chan', split_axis=0, concat_axis=1, tiled=True)]
    reduce_sum x1 -> x0, other arithmetic: 11.8 us -> none  [modal_tables(): jnp.sum(scaled_residue[:, None, :] * jnp.exp(-decay_rate[:, None, :] * po...]
    all_to_all x2 -> x0, local copies, waits for them, and re-layouts: 6.57 us -> none  [the longest x1 5.51 us: local(): lax.all_to_all(features, 'chan', split_axis=2, concat_axis=1, tiled=True)]
  transfers between devices with their start and end apart: 9 -> 0, of which waited for: 8 -> 0; matrix products, arithmetic and copies ran while one was open for 23% -> 0% of each run, Pallas kernels for 0% -> 0%
where the time goes in v1:
time: 32.9 us; the launch traced here: 32.5 us
  Pallas kernels  23.9 us (73%)
  local copies, waits for them, and re-layouts  8.59 us (26%)
    pallas_call x1, Pallas kernels, local(): pl.pallas_call(functools.partial(kernel, n_seq, n_chan, cores), out_shape...  23.9 us
    unnamed x17, local copies, waits for them, and re-layouts  8.59 us

profile of v1, /device:TPU:0, one launch (start us, length us, event | category | flops | bytes accessed | tf_op | source)
XLA Modules:
  0.0 32.5 jit_solution(17899656168744391385)
XLA Ops:
  0.0 0.0 copy-start
  0.0 1.9 %copy-done = bf16[3,128,4096]{2,1,0:T(8,128)(2,1)S(1)} copy-done((bf16[3,128,4096]{2,1,0:T(8,128)(2,1)S(1)}, bf16[3,128,4096]{2,1,0:T(8,128)(2,1)}, u32[]{:S(2)}) %copy-start) | copy-done | bytes 3145752
  1.9 0.0 copy-start.1
  1.9 0.9 %copy-done.1 = f32[3,3,4096]{2,1,0:T(4,128)S(1)} copy-done((f32[3,3,4096]{2,1,0:T(4,128)S(1)}, f32[3,3,4096]{2,1,0:T(4,128)}, u32[]{:S(2)}) %copy-start.1) | copy-done | bytes 147480
  2.8 0.0 copy-start.2
  2.8 0.8 %copy-done.2 = f32[16,1024]{1,0:T(8,128)S(1)} copy-done((f32[16,1024]{1,0:T(8,128)S(1)}, f32[16,1024]{1,0:T(8,128)}, u32[]{:S(2)}) %copy-start.2) | copy-done | bytes 65560
  3.7 0.0 copy-start.3
  3.7 0.8 %copy-done.3 = f32[16,1024]{1,0:T(8,128)S(1)} copy-done((f32[16,1024]{1,0:T(8,128)S(1)}, f32[16,1024]{1,0:T(8,128)}, u32[]{:S(2)}) %copy-start.3) | copy-done | bytes 65560
  4.5 0.0 copy-start.4
  4.5 0.7 %copy-done.4 = f32[1024]{0:T(1024)S(1)} copy-done((f32[1024]{0:T(1024)S(1)}, f32[1024]{0:T(1024)}, u32[]{:S(2)}) %copy-start.4) | copy-done | bytes 4120
  5.2 0.0 copy-start.5
  5.2 1.0 %copy-done.5 = bf16[128,1536]{1,0:T(8,128)(2,1)S(1)} copy-done((bf16[128,1536]{1,0:T(8,128)(2,1)S(1)}, bf16[128,1536]{1,0:T(8,128)(2,1)}, u32[]{:S(2)}) %copy-start.5) | copy-done | bytes 393240
  6.2 0.0 copy-start.6
  6.2 0.8 %copy-done.6 = bf16[128,16]{1,0:T(8,128)(2,1)S(1)} copy-done((bf16[128,16]{1,0:T(8,128)(2,1)S(1)}, bf16[128,16]{1,0:T(8,128)(2,1)}, u32[]{:S(2)}) %copy-start.6) | copy-done | bytes 4120
  6.9 0.0 copy-start.7
  6.9 0.7 %copy-done.7 = bf16[16,128]{1,0:T(8,128)(2,1)S(1)} copy-done((bf16[16,128]{1,0:T(8,128)(2,1)S(1)}, bf16[16,128]{1,0:T(8,128)(2,1)}, u32[]{:S(2)}) %copy-start.7) | copy-done | bytes 4120
  7.6 23.9 %shard_map.82 = bf16[128,4096]{1,0:T(8,128)(2,1)S(1)} custom-call(bf16[3,128,4096]{2,1,0:T(8,128)(2,1)S(1)} %copy-done, f32[3,3,4096]{2,1,0:T(4,128)S(1)} %copy-done.1, f32[16,1024]{1,0:T(8,128)S(1)} %copy-done.2, f32[16,1024]{1,0:T(8,128)S(1)} %copy-done.3, f32[1,1024]{1,0:T(1,128)S(1)} %bitcast.1, bf16[128,1536]{1,0:T(8,128)(2,1)S(1)} %copy-done.5, ...), custom_call_target="tpu_custom_call" | custom-call | flops 1610612736 | bytes 4194304 | tf_op jit(solution)/shard_map/pallas_call | solution.py:323
  31.5 1.0 %copy.10 = bf16[128,4096]{1,0:T(8,128)(2,1)} copy(bf16[128,4096]{1,0:T(8,128)(2,1)S(1)} %shard_map.82) | data formatting | bytes 2097152
Async XLA Ops:
  0.0 1.9 %copy-start = (bf16[3,128,4096]{2,1,0:T(8,128)(2,1)S(1)}, bf16[3,128,4096]{2,1,0:T(8,128)(2,1)}, u32[]{:S(2)}) copy-start(bf16[3,128,4096]{2,1,0:T(8,128)(2,1)} %feat_hbm.1) | copy-start | bytes 9437188
  1.9 0.9 %copy-start.1 = (f32[3,3,4096]{2,1,0:T(4,128)S(1)}, f32[3,3,4096]{2,1,0:T(4,128)}, u32[]{:S(2)}) copy-start(f32[3,3,4096]{2,1,0:T(4,128)} %taps.1) | copy-start | bytes 442372
  2.8 0.8 %copy-start.2 = (f32[16,1024]{1,0:T(8,128)S(1)}, f32[16,1024]{1,0:T(8,128)}, u32[]{:S(2)}) copy-start(f32[16,1024]{1,0:T(8,128)} %decay.1) | copy-start | bytes 196612
  3.7 0.8 %copy-start.3 = (f32[16,1024]{1,0:T(8,128)S(1)}, f32[16,1024]{1,0:T(8,128)}, u32[]{:S(2)}) copy-start(f32[16,1024]{1,0:T(8,128)} %residue.1) | copy-start | bytes 196612
  4.5 0.7 %copy-start.4 = (f32[1024]{0:T(1024)S(1)}, f32[1024]{0:T(1024)}, u32[]{:S(2)}) copy-start(f32[1024]{0:T(1024)} %param.12) | copy-start | bytes 12292
  5.2 1.0 %copy-start.5 = (bf16[128,1536]{1,0:T(8,128)(2,1)S(1)}, bf16[128,1536]{1,0:T(8,128)(2,1)}, u32[]{:S(2)}) copy-start(bf16[128,1536]{1,0:T(8,128)(2,1)} %constant.6.clone.toeplitz) | copy-start | bytes 1179652
  6.2 0.8 %copy-start.6 = (bf16[128,16]{1,0:T(8,128)(2,1)S(1)}, bf16[128,16]{1,0:T(8,128)(2,1)}, u32[]{:S(2)}) copy-start(bf16[128,16]{1,0:T(8,128)(2,1)} %constant.8.clone.basis) | copy-start | bytes 12292
  6.9 0.7 %copy-start.7 = (bf16[16,128]{1,0:T(8,128)(2,1)S(1)}, bf16[16,128]{1,0:T(8,128)(2,1)}, u32[]{:S(2)}) copy-start(bf16[16,128]{1,0:T(8,128)(2,1)} %constant.7.clone.moment) | copy-start | bytes 12292

commit v2 on v1

--- a/solution.py
+++ b/solution.py
@@ -42,10 +42,11 @@
 
 
 def kernel(
-    n_seq, n_chan, cores, feat_hbm, taps, decay, residue, skip, toeplitz, moment, basis, out,
-    feat, prod, gate, y, gx, modes, starts, border, b_send, b_recv,
+    n_seq, n_chan, cores, feat_hbm, taps_hbm, decay_hbm, residue_hbm, skip_hbm, toeplitz_hbm,
+    moment_hbm, basis_hbm, out,
+    feat, tail, taps, decay, residue, skip, toeplitz, moment, basis, prod, gate, y, gx, modes, starts, border, b_send, b_recv,
     g_all, m_send, m_recv, z_send, z_recv, h_send, h_recv,
-    copy_sem, b_ss, b_rs, g_ss, g_rs, m_ss, m_rs, h_ss, h_rs, z_ss, z_rs,
+    load_sem, store_sem, b_ss, b_rs, g_ss, g_rs, m_ss, m_rs, h_ss, h_rs, z_ss, z_rs,
 ):
     streams, block, width = feat.shape
     n_taps = taps.shape[1]
@@ -71,8 +72,18 @@
     def other(i):
         return lax.rem(me + i, members)
 
-    for m in range(streams):
-        pltpu.make_async_copy(feat_hbm.at[m], feat.at[m], copy_sem.at[m]).start()
+    own = pl.ds(pl.multiple_of(core * own_width, own_width), own_width)
+    places = [
+        (feat_hbm.at[:, pl.ds(block - 16, 16), :], tail),
+        (decay_hbm.at[:, own], decay), (residue_hbm.at[:, own], residue),
+        (skip_hbm.at[:, own], skip), (taps_hbm, taps),
+        (feat_hbm.at[1], feat.at[1]), (feat_hbm.at[2], feat.at[2]),
+        (moment_hbm, moment), (feat_hbm.at[0], feat.at[0]),
+        (toeplitz_hbm, toeplitz), (basis_hbm, basis),
+    ]
+    loads = [pltpu.make_async_copy(a, b, load_sem.at[k]) for k, (a, b) in enumerate(places)]
+    for load in loads:
+        load.start()
 
     barrier = pltpu.get_barrier_semaphore()
 
@@ -98,25 +109,10 @@
         pl.semaphore_signal(
             barrier, inc=1, device_id=((plane + 1) * cores, 0), device_id_type=MESH)
 
-    own = pl.ds(pl.multiple_of(core * own_width, own_width), own_width)
-    rate = decay[:, own]
-    scaled = residue[:, own] * jnp.sqrt(1.0 - jnp.exp(-2.0 * rate))
-    rows = []
-    for j in range(NODES):
-        a = jnp.exp(-rate * nodes[j])
-        modes[j] = a
-        rows.append(jnp.sum(scaled * a, axis=0, keepdims=True))
-    gain = skip[:, own]
-    gain_top = gain.astype(bf16).astype(f32)
-    rows += [gain_top, gain - gain_top]
-    rows += [jnp.zeros_like(gain)] * (ROWS - len(rows))
-    g_all[me] = jnp.concatenate(rows, axis=0).astype(bf16)
-
-    for m in range(streams):
-        pltpu.make_async_copy(feat_hbm.at[m], feat.at[m], copy_sem.at[m]).wait()
+    loads[0].wait()
     rows = []
     for m in range(streams):
-        last = feat[m, block - 16:, :].astype(f32)
+        last = tail[m].astype(f32)
         for k in range(n_taps - 1):
             row = 16 - (n_taps - 1) + k
             rows += [last[row:row + 1, f * fold:(f + 1) * fold] for f in range(folds)]
@@ -157,9 +153,52 @@
             src_ref=z_send, dst_ref=z_recv.at[slot], send_sem=z_ss.at[i],
             recv_sem=z_rs.at[slot], device_id=(i * cores + core, chan), device_id_type=MESH)
 
+    for load in loads[1:4]:
+        load.wait()
+    rate = decay[...]
+    scaled = residue[...] * jnp.sqrt(1.0 - jnp.exp(-2.0 * rate))
+    rows = []
+    for j in range(NODES):
+        a = jnp.exp(-rate * nodes[j])
+        modes[j] = a
+        rows.append(jnp.sum(scaled * a, axis=0, keepdims=True))
+    gain = skip[...]
+    gain_top = gain.astype(bf16).astype(f32)
+    rows += [gain_top, gain - gain_top]
+    rows += [jnp.zeros_like(gain)] * (ROWS - len(rows))
+    g_all[me] = jnp.concatenate(rows, axis=0).astype(bf16)
+
     @pl.loop(1, members)
     def _(i):
         g_copy(other(i), me).start()
+
+    top_row = lax.broadcasted_iota(jnp.int32, (8, own_width), 0)
+
+    def short_filter(m, cols, rows, with_border):
+        x = feat[m, :rows, cols].astype(f32)
+        total = taps[m, 0:1, cols] * x
+        for j in range(1, n_taps):
+            moved = pltpu.roll(x, j, 0)
+            if with_border:
+                top = moved[:8]
+                for k in range(j):
+                    place = m * (n_taps - 1) + n_taps - 1 - j + k
+                    top = jnp.where(top_row == k, border[place:place + 1, cols], top)
+                moved = jnp.concatenate([top, moved[8:]], axis=0)
+            total = total + taps[m, j:j + 1, cols] * moved
+        return total.astype(bf16)
+
+    def product(cols, rows, with_border):
+        left = short_filter(1, cols, rows, with_border).astype(f32)
+        return (left * short_filter(2, cols, rows, with_border).astype(f32)).astype(bf16)
+
+    for load in loads[4:7]:
+        load.wait()
+
+    @pl.loop(0, members)
+    def _(i):
+        cols = columns(i)
+        prod[:, cols] = product(cols, block, False)
 
     @pl.when(position > 0)
     def _():
@@ -176,28 +215,14 @@
     def _():
         border[...] = jnp.zeros_like(border)
 
-    top_row = lax.broadcasted_iota(jnp.int32, (8, own_width), 0)
-
-    def short_filter(m, cols):
-        x = feat[m, :, cols].astype(f32)
-        total = taps[m, 0:1, cols] * x
-        for j in range(1, n_taps):
-            moved = pltpu.roll(x, j, 0)
-            top = moved[:8]
-            for k in range(j):
-                place = m * (n_taps - 1) + n_taps - 1 - j + k
-                top = jnp.where(top_row == k, border[place:place + 1, cols], top)
-            moved = jnp.concatenate([top, moved[8:]], axis=0)
-            total = total + taps[m, j:j + 1, cols] * moved
-        return total.astype(bf16)
+    loads[7].wait()
 
     @pl.loop(1, members + 1)
     def _(i):
         to = other(i)
         cols = columns(to)
-        p = (short_filter(1, cols).astype(f32) * short_filter(2, cols).astype(f32)).astype(bf16)
-        prod[:, cols] = p
-        found = jnp.dot(moment[...], p, preferred_element_type=f32).astype(bf16)
+        prod[:16, cols] = product(cols, 16, True)
+        found = jnp.dot(moment[...], prod[:, cols], preferred_element_type=f32).astype(bf16)
 
         @pl.when(i < members)
         def _():
@@ -208,10 +233,12 @@
         def _():
             m_recv[me] = found
 
+    loads[8].wait()
+
     @pl.loop(0, members)
     def _(i):
         cols = columns(i)
-        gate[:, cols] = short_filter(0, cols)
+        gate[:, cols] = short_filter(0, cols, block, True)
 
     block_decay = jnp.exp(-rate * block)
 
@@ -238,8 +265,9 @@
     def _(i):
         g_copy(other(i), other(i)).wait_recv()
 
-    @pl.loop(0, members)
-    def _(i):
+    loads[9].wait()
+
+    def own_part(i):
         cols = columns(i)
         p = prod[:, cols]
         g = g_all[i].astype(f32)
@@ -250,6 +278,12 @@
         both = g[NODES:NODES + 1] + g[NODES + 1:NODES + 2]
         y[:, cols] = inner + both * p.astype(f32)
 
+    early = members // 2
+
+    @pl.loop(0, early)
+    def _(i):
+        own_part(i)
+
     plane_decay = jnp.exp(-rate * (block * members))
 
     def gather_plane(i, state):
@@ -278,6 +312,16 @@
 
     lax.fori_loop(0, members, respond, entering)
 
+    @pl.loop(early, members)
+    def _(i):
+        own_part(i)
+
+    loads[10].wait()
+
+    def store(i):
+        return pltpu.make_async_copy(
+            gate.at[:, columns(i)], out.at[:, columns(i)], store_sem.at[i])
+
     @pl.loop(0, members)
     def _(i):
         at = other(i)
@@ -289,7 +333,8 @@
 
         carried = jnp.dot(basis[...], h_recv[at], preferred_element_type=f32)
         conv = (y[:, cols] + carried).astype(bf16)
-        out[:, cols] = (gate[:, cols].astype(f32) * conv.astype(f32)).astype(bf16)
+        gate[:, cols] = (gate[:, cols].astype(f32) * conv.astype(f32)).astype(bf16)
+        store(at).start()
 
     @pl.when(position < total - 1)
     def _():
@@ -304,6 +349,10 @@
     @pl.loop(plane + 1, planes)
     def _(i):
         z_copy(i, plane).wait_send()
+
+    @pl.loop(0, members)
+    def _(i):
+        store(i).wait()
 
 
 def local(n_seq, n_chan, features, short_weight, decay_rate, residue, skip_gain):
@@ -317,16 +366,24 @@
     fold = width // 4
     halo_rows = -(-halo * 4 // 16) * 16
     toeplitz, moment, basis = constant_tables(block)
-    vmem = pl.BlockSpec(memory_space=pltpu.VMEM)
+    anywhere = pl.BlockSpec(memory_space=pl.ANY)
     dma = pltpu.SemaphoreType.DMA
     small = pltpu.VMEM((members, ROWS, own_width), bf16)
     return pl.pallas_call(
         functools.partial(kernel, n_seq, n_chan, cores),
         out_shape=jax.ShapeDtypeStruct((block, width), bf16),
-        in_specs=[pl.BlockSpec(memory_space=pl.ANY)] + [vmem] * 7,
-        out_specs=vmem,
+        in_specs=[anywhere] * 8,
+        out_specs=anywhere,
         scratch_shapes=[
             pltpu.VMEM((streams, block, width), bf16),
+            pltpu.VMEM((streams, 16, width), bf16),
+            pltpu.VMEM(short_weight.shape, f32),
+            pltpu.VMEM((modes, own_width), f32),
+            pltpu.VMEM((modes, own_width), f32),
+            pltpu.VMEM((1, own_width), f32),
+            pltpu.VMEM(toeplitz.shape, bf16),
+            pltpu.VMEM(moment.shape, bf16),
+            pltpu.VMEM(basis.shape, bf16),
             pltpu.VMEM((block, width), bf16),
             pltpu.VMEM((block, width), bf16),
             pltpu.VMEM((block, width), f32),
@@ -340,12 +397,12 @@
             pltpu.VMEM((modes, own_width), bf16),
             pltpu.VMEM((planes, modes, own_width), bf16),
             small, small,
-            dma((streams,)), dma, dma,
+            dma((11,)), dma((members,)), dma, dma,
             dma((members,)), dma((members,)), dma((members,)), dma((members,)),
             dma((members,)), dma((members,)), dma((planes,)), dma((planes,)),
         ],
         compiler_params=pltpu.CompilerParams(
-            collective_id=0, has_side_effects=True, vmem_limit_bytes=40 * 2**20),
+            collective_id=0, has_side_effects=True, vmem_limit_bytes=60 * 2**20),
         cost_estimate=pl.CostEstimate(
             flops=2 * block * NODES * block * width,
             bytes_accessed=8 * block * width, transcendentals=0),

time: 32.9 us -> 23.9 us (0.73)
  local copies, waits for them, and re-layouts: 8.59 us -> 2.29 us
  Pallas kernels: 23.9 us -> 21.5 us
    unnamed x17 -> x1, local copies, waits for them, and re-layouts: 8.59 us -> 2.29 us
    pallas_call x1, Pallas kernels: 23.9 us -> 21.5 us  [local(): pl.pallas_call(functools.partial(kernel, n_seq, n_chan, cores), out_shape...]
where the time goes in v2:
time: 23.9 us; the launch traced here: 23.8 us
  Pallas kernels  21.5 us (90%)
  local copies, waits for them, and re-layouts  2.29 us (10%)
    pallas_call x1, Pallas kernels, local(): pl.pallas_call(functools.partial(kernel, n_seq, n_chan, cores), out_shape...  21.5 us
    unnamed x1, local copies, waits for them, and re-layouts  2.29 us

profile of v2, /device:TPU:0, one launch (start us, length us, event | category | flops | bytes accessed | tf_op | source)
XLA Modules:
  0.0 23.8 jit_solution(2111495085561118887)
XLA Ops:
  0.0 21.5 %shard_map.82 = bf16[128,4096]{1,0:T(8,128)(2,1)} custom-call(bf16[3,128,4096]{2,1,0:T(8,128)(2,1)} %feat_hbm.1, f32[3,3,4096]{2,1,0:T(4,128)} %taps_hbm.1, f32[16,1024]{1,0:T(8,128)} %decay_hbm.1, f32[16,1024]{1,0:T(8,128)} %residue_hbm.1, f32[1,1024]{1,0:T(1,128)} %bitcast.1, bf16[128,1536]{1,0:T(8,128)(2,1)} %constant.6.clone.toeplitz_hbm, ...), custom_call_target="tpu_custom_call" | custom-call | flops 1610612736 | bytes 4194304 | tf_op jit(solution)/shard_map/pallas_call | solution.py:372
  21.5 2.3 %copy.10 = bf16[128,4096]{1,0:T(8,128)(2,1)} copy(bf16[128,4096]{1,0:T(8,128)(2,1)} %shard_map.82) | data formatting | bytes 2097152

commit v3 on v2

--- a/solution.py
+++ b/solution.py
@@ -46,7 +46,7 @@
     moment_hbm, basis_hbm, out,
     feat, tail, taps, decay, residue, skip, toeplitz, moment, basis, prod, gate, y, gx, modes, starts, border, b_send, b_recv,
     g_all, m_send, m_recv, z_send, z_recv, h_send, h_recv,
-    load_sem, store_sem, b_ss, b_rs, g_ss, g_rs, m_ss, m_rs, h_ss, h_rs, z_ss, z_rs,
+    load_sem, b_ss, b_rs, g_ss, g_rs, m_ss, m_rs, h_ss, h_rs, z_ss, z_rs,
 ):
     streams, block, width = feat.shape
     n_taps = taps.shape[1]
@@ -318,10 +318,6 @@
 
     loads[10].wait()
 
-    def store(i):
-        return pltpu.make_async_copy(
-            gate.at[:, columns(i)], out.at[:, columns(i)], store_sem.at[i])
-
     @pl.loop(0, members)
     def _(i):
         at = other(i)
@@ -333,8 +329,7 @@
 
         carried = jnp.dot(basis[...], h_recv[at], preferred_element_type=f32)
         conv = (y[:, cols] + carried).astype(bf16)
-        gate[:, cols] = (gate[:, cols].astype(f32) * conv.astype(f32)).astype(bf16)
-        store(at).start()
+        out[:, cols] = (gate[:, cols].astype(f32) * conv.astype(f32)).astype(bf16)
 
     @pl.when(position < total - 1)
     def _():
@@ -349,10 +344,6 @@
     @pl.loop(plane + 1, planes)
     def _(i):
         z_copy(i, plane).wait_send()
-
-    @pl.loop(0, members)
-    def _(i):
-        store(i).wait()
 
 
 def local(n_seq, n_chan, features, short_weight, decay_rate, residue, skip_gain):
@@ -371,9 +362,9 @@
     small = pltpu.VMEM((members, ROWS, own_width), bf16)
     return pl.pallas_call(
         functools.partial(kernel, n_seq, n_chan, cores),
-        out_shape=jax.ShapeDtypeStruct((block, width), bf16),
+        out_shape=pltpu.VMEM((block, width), bf16),
         in_specs=[anywhere] * 8,
-        out_specs=anywhere,
+        out_specs=pl.BlockSpec(memory_space=pltpu.VMEM),
         scratch_shapes=[
             pltpu.VMEM((streams, block, width), bf16),
             pltpu.VMEM((streams, 16, width), bf16),
@@ -397,7 +388,7 @@
             pltpu.VMEM((modes, own_width), bf16),
             pltpu.VMEM((planes, modes, own_width), bf16),
             small, small,
-            dma((11,)), dma((members,)), dma, dma,
+            dma((11,)), dma, dma,
             dma((members,)), dma((members,)), dma((members,)), dma((members,)),
             dma((members,)), dma((members,)), dma((planes,)), dma((planes,)),
         ],

time: 23.9 us -> 22 us (0.921)
  local copies, waits for them, and re-layouts: 2.29 us -> 0.97 us
  Pallas kernels: 21.5 us -> 20.9 us
    unnamed x1, local copies, waits for them, and re-layouts: 2.29 us -> 0.97 us
    pallas_call x1, Pallas kernels: 21.5 us -> 20.9 us  [local(): pl.pallas_call(functools.partial(kernel, n_seq, n_chan, cores), out_shape...]
where the time goes in v3:
time: 22 us; the launch traced here: 21.8 us
  Pallas kernels  20.9 us (95%)
  local copies, waits for them, and re-layouts  0.97 us (4%)
    pallas_call x1, Pallas kernels, local(): pl.pallas_call(functools.partial(kernel, n_seq, n_chan, cores), out_shape...  20.9 us
    unnamed x1, local copies, waits for them, and re-layouts  0.97 us

profile of v3, /device:TPU:0, one launch (start us, length us, event | category | flops | bytes accessed | tf_op | source)
XLA Modules:
  0.0 21.8 jit_solution(1530443810265774511)
XLA Ops:
  0.0 20.9 %shard_map.82 = bf16[128,4096]{1,0:T(8,128)(2,1)S(1)} custom-call(bf16[3,128,4096]{2,1,0:T(8,128)(2,1)} %feat_hbm.1, f32[3,3,4096]{2,1,0:T(4,128)} %taps_hbm.1, f32[16,1024]{1,0:T(8,128)} %decay_hbm.1, f32[16,1024]{1,0:T(8,128)} %residue_hbm.1, f32[1,1024]{1,0:T(1,128)} %bitcast.1, bf16[128,1536]{1,0:T(8,128)(2,1)} %constant.6.clone.toeplitz_hbm, ...), custom_call_target="tpu_custom_call" | custom-call | flops 1610612736 | bytes 4194304 | tf_op jit(solution)/shard_map/pallas_call | solution.py:363
  20.9 1.0 %copy.10 = bf16[128,4096]{1,0:T(8,128)(2,1)} copy(bf16[128,4096]{1,0:T(8,128)(2,1)S(1)} %shard_map.82) | data formatting | bytes 2097152

commit v4 on v3

--- a/solution.py
+++ b/solution.py
@@ -13,6 +13,7 @@
 
 NODES = 12
 ROWS = 16
+LANES = 128
 
 
 def node_places(block):
@@ -69,6 +70,11 @@
         start = lax.rem(i, n_chan) * chan_width + (i // n_chan) * own_width
         return pl.ds(pl.multiple_of(start, own_width), own_width)
 
+    def strips(i):
+        start = lax.rem(i, n_chan) * chan_width + (i // n_chan) * own_width
+        for k in range(0, own_width, LANES):
+            yield pl.ds(pl.multiple_of(start + k, LANES), LANES)
+
     def other(i):
         return lax.rem(me + i, members)
 
@@ -172,7 +178,7 @@
     def _(i):
         g_copy(other(i), me).start()
 
-    top_row = lax.broadcasted_iota(jnp.int32, (8, own_width), 0)
+    top_row = lax.broadcasted_iota(jnp.int32, (8, LANES), 0)
 
     def short_filter(m, cols, rows, with_border):
         x = feat[m, :rows, cols].astype(f32)
@@ -197,8 +203,8 @@
 
     @pl.loop(0, members)
     def _(i):
-        cols = columns(i)
-        prod[:, cols] = product(cols, block, False)
+        for cols in strips(i):
+            prod[:, cols] = product(cols, block, False)
 
     @pl.when(position > 0)
     def _():
@@ -220,9 +226,9 @@
     @pl.loop(1, members + 1)
     def _(i):
         to = other(i)
-        cols = columns(to)
-        prod[:16, cols] = product(cols, 16, True)
-        found = jnp.dot(moment[...], prod[:, cols], preferred_element_type=f32).astype(bf16)
+        for cols in strips(to):
+            prod[:16, cols] = product(cols, 16, True)
+        found = jnp.dot(moment[...], prod[:, columns(to)], preferred_element_type=f32).astype(bf16)
 
         @pl.when(i < members)
         def _():
@@ -237,8 +243,8 @@
 
     @pl.loop(0, members)
     def _(i):
-        cols = columns(i)
-        gate[:, cols] = short_filter(0, cols, block, True)
+        for cols in strips(i):
+            gate[:, cols] = short_filter(0, cols, block, True)
 
     block_decay = jnp.exp(-rate * block)
 
@@ -321,15 +327,15 @@
     @pl.loop(0, members)
     def _(i):
         at = other(i)
-        cols = columns(at)
-
         @pl.when(i > 0)
         def _():
             h_copy(at, at).wait_recv()
 
-        carried = jnp.dot(basis[...], h_recv[at], preferred_element_type=f32)
-        conv = (y[:, cols] + carried).astype(bf16)
-        out[:, cols] = (gate[:, cols].astype(f32) * conv.astype(f32)).astype(bf16)
+        for k, cols in enumerate(strips(at)):
+            answer = h_recv[at, :, k * LANES:(k + 1) * LANES]
+            carried = jnp.dot(basis[...], answer, preferred_element_type=f32)
+            conv = (y[:, cols] + carried).astype(bf16)
+            out[:, cols] = (gate[:, cols].astype(f32) * conv.astype(f32)).astype(bf16)
 
     @pl.when(position < total - 1)
     def _():

time: 22 us -> 22.1 us (level)
  no operation moved by 1% of the time
where the time goes in v4:
time: 22.1 us; the launch traced here: 22 us
  Pallas kernels  21 us (95%)
  local copies, waits for them, and re-layouts  0.97 us (4%)
    pallas_call x1, Pallas kernels, local(): pl.pallas_call(functools.partial(kernel, n_seq, n_chan, cores), out_shape...  21 us
    unnamed x1, local copies, waits for them, and re-layouts  0.97 us

profile of v4, /device:TPU:0, one launch (start us, length us, event | category | flops | bytes accessed | tf_op | source)
XLA Modules:
  0.0 22.0 jit_solution(487537080039538159)
XLA Ops:
  0.0 21.0 %shard_map.82 = bf16[128,4096]{1,0:T(8,128)(2,1)S(1)} custom-call(bf16[3,128,4096]{2,1,0:T(8,128)(2,1)} %feat_hbm.1, f32[3,3,4096]{2,1,0:T(4,128)} %taps_hbm.1, f32[16,1024]{1,0:T(8,128)} %decay_hbm.1, f32[16,1024]{1,0:T(8,128)} %residue_hbm.1, f32[1,1024]{1,0:T(1,128)} %bitcast.1, bf16[128,1536]{1,0:T(8,128)(2,1)} %constant.6.clone.toeplitz_hbm, ...), custom_call_target="tpu_custom_call" | custom-call | flops 1610612736 | bytes 4194304 | tf_op jit(solution)/shard_map/pallas_call | solution.py:369
  21.0 1.0 %copy.10 = bf16[128,4096]{1,0:T(8,128)(2,1)} copy(bf16[128,4096]{1,0:T(8,128)(2,1)S(1)} %shard_map.82) | data formatting | bytes 2097152

commit v5 on v4

--- a/solution.py
+++ b/solution.py
@@ -125,40 +125,6 @@
     rows += [jnp.zeros_like(rows[0])] * (b_send.shape[0] - len(rows))
     b_send[...] = jnp.concatenate(rows, axis=0).astype(bf16)
 
-    extra = jnp.where(enters, 1, 0) + jnp.where(leaves, 1, 0)
-    pl.semaphore_wait(barrier, members - 1 + planes - 1 + extra)
-
-    position = seq * n_chan + chan
-    total = n_seq * n_chan
-    after = lax.rem(position + 1, total)
-    b_copy = pltpu.make_async_remote_copy(
-        src_ref=b_send, dst_ref=b_recv, send_sem=b_ss, recv_sem=b_rs,
-        device_id=(after // n_chan, lax.rem(after, n_chan)), device_id_type=MESH)
-
-    @pl.when(position < total - 1)
-    def _():
-        b_copy.start()
-
-    def g_copy(i, slot):
-        return pltpu.make_async_remote_copy(
-            src_ref=g_all.at[slot], dst_ref=g_all.at[slot], send_sem=g_ss.at[i],
-            recv_sem=g_rs.at[slot], device_id=member(i), device_id_type=MESH)
-
-    def m_copy(i, slot):
-        return pltpu.make_async_remote_copy(
-            src_ref=m_send.at[i], dst_ref=m_recv.at[slot], send_sem=m_ss.at[i],
-            recv_sem=m_rs.at[slot], device_id=member(i), device_id_type=MESH)
-
-    def h_copy(i, slot):
-        return pltpu.make_async_remote_copy(
-            src_ref=h_send.at[i], dst_ref=h_recv.at[slot], send_sem=h_ss.at[i],
-            recv_sem=h_rs.at[slot], device_id=member(i), device_id_type=MESH)
-
-    def z_copy(i, slot):
-        return pltpu.make_async_remote_copy(
-            src_ref=z_send, dst_ref=z_recv.at[slot], send_sem=z_ss.at[i],
-            recv_sem=z_rs.at[slot], device_id=(i * cores + core, chan), device_id_type=MESH)
-
     for load in loads[1:4]:
         load.wait()
     rate = decay[...]
@@ -174,6 +140,40 @@
     rows += [jnp.zeros_like(gain)] * (ROWS - len(rows))
     g_all[me] = jnp.concatenate(rows, axis=0).astype(bf16)
 
+    extra = jnp.where(enters, 1, 0) + jnp.where(leaves, 1, 0)
+    pl.semaphore_wait(barrier, members - 1 + planes - 1 + extra)
+
+    position = seq * n_chan + chan
+    total = n_seq * n_chan
+    after = lax.rem(position + 1, total)
+    b_copy = pltpu.make_async_remote_copy(
+        src_ref=b_send, dst_ref=b_recv, send_sem=b_ss, recv_sem=b_rs,
+        device_id=(after // n_chan, lax.rem(after, n_chan)), device_id_type=MESH)
+
+    @pl.when(position < total - 1)
+    def _():
+        b_copy.start()
+
+    def g_copy(i, slot):
+        return pltpu.make_async_remote_copy(
+            src_ref=g_all.at[slot], dst_ref=g_all.at[slot], send_sem=g_ss.at[i],
+            recv_sem=g_rs.at[slot], device_id=member(i), device_id_type=MESH)
+
+    def m_copy(i, slot):
+        return pltpu.make_async_remote_copy(
+            src_ref=m_send.at[i], dst_ref=m_recv.at[slot], send_sem=m_ss.at[i],
+            recv_sem=m_rs.at[slot], device_id=member(i), device_id_type=MESH)
+
+    def h_copy(i, slot):
+        return pltpu.make_async_remote_copy(
+            src_ref=h_send.at[i], dst_ref=h_recv.at[slot], send_sem=h_ss.at[i],
+            recv_sem=h_rs.at[slot], device_id=member(i), device_id_type=MESH)
+
+    def z_copy(i, slot):
+        return pltpu.make_async_remote_copy(
+            src_ref=z_send, dst_ref=z_recv.at[slot], send_sem=z_ss.at[i],
+            recv_sem=z_rs.at[slot], device_id=(i * cores + core, chan), device_id_type=MESH)
+
     @pl.loop(1, members)
     def _(i):
         g_copy(other(i), me).start()
@@ -278,8 +278,9 @@
         p = prod[:, cols]
         g = g_all[i].astype(f32)
         for j in range(NODES):
-            gx[j * block:(j + 1) * block, :] = (
-                jnp.broadcast_to(g[j:j + 1], p.shape).astype(bf16) * p)
+            row = jnp.broadcast_to(g[j:j + 1], (16, own_width)).astype(bf16)
+            for r in range(0, block, 16):
+                gx[j * block + r:j * block + r + 16, :] = row * p[r:r + 16]
         inner = jnp.dot(toeplitz[...], gx[...], preferred_element_type=f32)
         both = g[NODES:NODES + 1] + g[NODES + 1:NODES + 2]
         y[:, cols] = inner + both * p.astype(f32)

time: 22.1 us -> 22.1 us (level)
  no operation moved by 1% of the time
where the time goes in v5:
time: 22.1 us; the launch traced here: 22 us
  Pallas kernels  21 us (95%)
  local copies, waits for them, and re-layouts  0.97 us (4%)
    pallas_call x1, Pallas kernels, local(): pl.pallas_call(functools.partial(kernel, n_seq, n_chan, cores), out_shape...  21 us
    unnamed x1, local copies, waits for them, and re-layouts  0.97 us

profile of v5, /device:TPU:0, one launch (start us, length us, event | category | flops | bytes accessed | tf_op | source)
XLA Modules:
  0.0 22.0 jit_solution(18002273017666224673)
XLA Ops:
  0.0 21.0 %shard_map.82 = bf16[128,4096]{1,0:T(8,128)(2,1)S(1)} custom-call(bf16[3,128,4096]{2,1,0:T(8,128)(2,1)} %feat_hbm.1, f32[3,3,4096]{2,1,0:T(4,128)} %taps_hbm.1, f32[16,1024]{1,0:T(8,128)} %decay_hbm.1, f32[16,1024]{1,0:T(8,128)} %residue_hbm.1, f32[1,1024]{1,0:T(1,128)} %bitcast.1, bf16[128,1536]{1,0:T(8,128)(2,1)} %constant.6.clone.toeplitz_hbm, ...), custom_call_target="tpu_custom_call" | custom-call | flops 1610612736 | bytes 4194304 | tf_op jit(solution)/shard_map/pallas_call | solution.py:370
  21.0 1.0 %copy.10 = bf16[128,4096]{1,0:T(8,128)(2,1)} copy(bf16[128,4096]{1,0:T(8,128)(2,1)S(1)} %shard_map.82) | data formatting | bytes 2097152

commit v6 on v5

--- a/solution.py
+++ b/solution.py
@@ -140,44 +140,6 @@
     rows += [jnp.zeros_like(gain)] * (ROWS - len(rows))
     g_all[me] = jnp.concatenate(rows, axis=0).astype(bf16)
 
-    extra = jnp.where(enters, 1, 0) + jnp.where(leaves, 1, 0)
-    pl.semaphore_wait(barrier, members - 1 + planes - 1 + extra)
-
-    position = seq * n_chan + chan
-    total = n_seq * n_chan
-    after = lax.rem(position + 1, total)
-    b_copy = pltpu.make_async_remote_copy(
-        src_ref=b_send, dst_ref=b_recv, send_sem=b_ss, recv_sem=b_rs,
-        device_id=(after // n_chan, lax.rem(after, n_chan)), device_id_type=MESH)
-
-    @pl.when(position < total - 1)
-    def _():
-        b_copy.start()
-
-    def g_copy(i, slot):
-        return pltpu.make_async_remote_copy(
-            src_ref=g_all.at[slot], dst_ref=g_all.at[slot], send_sem=g_ss.at[i],
-            recv_sem=g_rs.at[slot], device_id=member(i), device_id_type=MESH)
-
-    def m_copy(i, slot):
-        return pltpu.make_async_remote_copy(
-            src_ref=m_send.at[i], dst_ref=m_recv.at[slot], send_sem=m_ss.at[i],
-            recv_sem=m_rs.at[slot], device_id=member(i), device_id_type=MESH)
-
-    def h_copy(i, slot):
-        return pltpu.make_async_remote_copy(
-            src_ref=h_send.at[i], dst_ref=h_recv.at[slot], send_sem=h_ss.at[i],
-            recv_sem=h_rs.at[slot], device_id=member(i), device_id_type=MESH)
-
-    def z_copy(i, slot):
-        return pltpu.make_async_remote_copy(
-            src_ref=z_send, dst_ref=z_recv.at[slot], send_sem=z_ss.at[i],
-            recv_sem=z_rs.at[slot], device_id=(i * cores + core, chan), device_id_type=MESH)
-
-    @pl.loop(1, members)
-    def _(i):
-        g_copy(other(i), me).start()
-
     top_row = lax.broadcasted_iota(jnp.int32, (8, LANES), 0)
 
     def short_filter(m, cols, rows, with_border):
@@ -201,7 +163,52 @@
     for load in loads[4:7]:
         load.wait()
 
-    @pl.loop(0, members)
+    half = members // 2
+
+    @pl.loop(0, half)
+    def _(i):
+        for cols in strips(i):
+            prod[:, cols] = product(cols, block, False)
+
+    extra = jnp.where(enters, 1, 0) + jnp.where(leaves, 1, 0)
+    pl.semaphore_wait(barrier, members - 1 + planes - 1 + extra)
+
+    position = seq * n_chan + chan
+    total = n_seq * n_chan
+    after = lax.rem(position + 1, total)
+    b_copy = pltpu.make_async_remote_copy(
+        src_ref=b_send, dst_ref=b_recv, send_sem=b_ss, recv_sem=b_rs,
+        device_id=(after // n_chan, lax.rem(after, n_chan)), device_id_type=MESH)
+
+    @pl.when(position < total - 1)
+    def _():
+        b_copy.start()
+
+    def g_copy(i, slot):
+        return pltpu.make_async_remote_copy(
+            src_ref=g_all.at[slot], dst_ref=g_all.at[slot], send_sem=g_ss.at[i],
+            recv_sem=g_rs.at[slot], device_id=member(i), device_id_type=MESH)
+
+    def m_copy(i, slot):
+        return pltpu.make_async_remote_copy(
+            src_ref=m_send.at[i], dst_ref=m_recv.at[slot], send_sem=m_ss.at[i],
+            recv_sem=m_rs.at[slot], device_id=member(i), device_id_type=MESH)
+
+    def h_copy(i, slot):
+        return pltpu.make_async_remote_copy(
+            src_ref=h_send.at[i], dst_ref=h_recv.at[slot], send_sem=h_ss.at[i],
+            recv_sem=h_rs.at[slot], device_id=member(i), device_id_type=MESH)
+
+    def z_copy(i, slot):
+        return pltpu.make_async_remote_copy(
+            src_ref=z_send, dst_ref=z_recv.at[slot], send_sem=z_ss.at[i],
+            recv_sem=z_rs.at[slot], device_id=(i * cores + core, chan), device_id_type=MESH)
+
+    @pl.loop(1, members)
+    def _(i):
+        g_copy(other(i), me).start()
+
+    @pl.loop(half, members)
     def _(i):
         for cols in strips(i):
             prod[:, cols] = product(cols, block, False)

time: 22.1 us -> 22.2 us (level)
  no operation moved by 1% of the time
where the time goes in v6:
time: 22.2 us; the launch traced here: 22 us
  Pallas kernels  21 us (95%)
  local copies, waits for them, and re-layouts  0.97 us (4%)
    pallas_call x1, Pallas kernels, local(): pl.pallas_call(functools.partial(kernel, n_seq, n_chan, cores), out_shape...  21 us
    unnamed x1, local copies, waits for them, and re-layouts  0.97 us

profile of v6, /device:TPU:0, one launch (start us, length us, event | category | flops | bytes accessed | tf_op | source)
XLA Modules:
  0.0 22.0 jit_solution(8267861664268265705)
XLA Ops:
  0.0 21.0 %shard_map.82 = bf16[128,4096]{1,0:T(8,128)(2,1)S(1)} custom-call(bf16[3,128,4096]{2,1,0:T(8,128)(2,1)} %feat_hbm.1, f32[3,3,4096]{2,1,0:T(4,128)} %taps_hbm.1, f32[16,1024]{1,0:T(8,128)} %decay_hbm.1, f32[16,1024]{1,0:T(8,128)} %residue_hbm.1, f32[1,1024]{1,0:T(1,128)} %bitcast.1, bf16[128,1536]{1,0:T(8,128)(2,1)} %constant.6.clone.toeplitz_hbm, ...), custom_call_target="tpu_custom_call" | custom-call | flops 1610612736 | bytes 4194304 | tf_op jit(solution)/shard_map/pallas_call | solution.py:377
  21.1 1.0 %copy.10 = bf16[128,4096]{1,0:T(8,128)(2,1)} copy(bf16[128,4096]{1,0:T(8,128)(2,1)S(1)} %shard_map.82) | data formatting | bytes 2097152
